TPU v7x, 32 devices: a whole 2x2x4 slice. The times are simulated.
32 devices in a mesh: clips: 2 (over y), ha: 4 (over z), wa: 2 (over core), ta: 2 (over x).
Axes of the slice: x: 2, y: 2, z: 4, core: 2. Of those that a mesh axis runs over, the one named last changes fastest.
Arguments:
- frames: bfloat16 [8, 16, 256, 128], P(('clips', 'ta'), 'ha', 'wa'), parts along dimension 0, may hold values from -12 to 12
- past_first: bfloat16 [4, 16, 256, 128], P('clips', 'ha', 'wa'), parts along dimension 0, may hold values from -6 to 6
- past_second: bfloat16 [4, 16, 256, 128], P('clips', 'ha', 'wa'), parts along dimension 0, may hold values from -6 to 6
- gain_first: float32 [128], replicated, may hold values from 0.5 to 1.5
- shift_first: float32 [128], replicated, may hold values from -3 to 3
- kernel_first: bfloat16 [3, 3, 3, 128, 128], replicated, may hold values from -0.109375 to 0.109375
- bias_first: float32 [128], replicated, may hold values from -2 to 2
- gain_second: float32 [128], replicated, may hold values from 0.5 to 1.5
- shift_second: float32 [128], replicated, may hold values from -3 to 3
- kernel_second: bfloat16 [3, 3, 3, 128, 128], replicated, may hold values from -0.109375 to 0.109375
- bias_second: float32 [128], replicated, may hold values from -2 to 2
Outputs:
- decoded: bfloat16 [8, 16, 256, 128], P(('clips', 'ta'), 'ha', 'wa'), parts along dimension 0
There are 2 independent parts, one for each index of `clips`. A program takes and returns all parts, laid end to end along the dimension named above; an argument that names none is the same for every part. Nothing has to cross between parts.
All inputs are finite; a program needn't handle non-finite values.
Results may differ from a plain program's by a relative error of at most 0.0039.
Values may be sent and summed in bfloat16 or wider, within the bound.
A program may use at most 64 MiB of HBM per device.

v0:
```python
import functools

import jax
import jax.numpy as jnp
from jax import lax
from jax.experimental import pallas as pl
from jax.experimental.pallas import tpu as pltpu
from jax.sharding import PartitionSpec as P

EPS = 1e-06
G = 32
PAD = 16
MESH = pl.DeviceIdType.MESH
DIRECTIONS = [(dh, dw) for dh in (-1, 0, 1) for dw in (-1, 0, 1) if (dh, dw) != (0, 0)]


def body(
    sizes,
    frames,
    past_first,
    past_second,
    gain_first_in,
    shift_first_in,
    kernel_first,
    bias_first_in,
    gain_second_in,
    shift_second_in,
    kernel_second,
    bias_second_in,
    out,
    vectors,
    total,
    raw,
    hid_edge,
    hid,
    line,
    cols_one,
    cols_two,
    weight_one,
    weight_two,
    stat_own,
    stat_in,
    local_sem,
    raw_send,
    raw_recv,
    hid_send,
    hid_recv,
    time_send,
    time_recv,
    stat_send,
    stat_recv,
):
    nha, nwa, nta = sizes
    peers = nha * nwa * nta
    _, nframe, rows2, width, chans = raw.shape
    rows, cols = rows2 - 2, width - 2 * PAD
    ha, wa, ta = lax.axis_index("ha"), lax.axis_index("wa"), lax.axis_index("ta")
    me = (ha * nwa + wa) * nta + ta
    count = float(nframe * rows * cols * (chans // G) * peers)

    def place(k):
        other = lax.rem(me + k, peers)
        return {
            "ha": other // (nwa * nta),
            "wa": lax.rem(other // nta, nwa),
            "ta": lax.rem(other, nta),
        }

    def inner(buf, slot):
        return buf.at[slot, :, pl.ds(1, rows), pl.ds(PAD, cols), :]

    load_frames = pltpu.make_async_copy(frames, inner(raw, 2), local_sem.at[0])
    load_past = pltpu.make_async_copy(past_first, inner(raw, jnp.maximum(1 - ta, 0)), local_sem.at[1])
    load_second = pltpu.make_async_copy(past_second, inner(hid_edge, 0), local_sem.at[2])
    vector_in = (
        gain_first_in,
        shift_first_in,
        bias_first_in,
        gain_second_in,
        shift_second_in,
        bias_second_in,
    )
    load_vectors = [
        pltpu.make_async_copy(ref, vectors.at[i], local_sem.at[5 + i])
        for i, ref in enumerate(vector_in)
    ]
    gain_first, shift_first, bias_first, gain_second, shift_second, bias_second = (
        vectors.at[i] for i in range(6)
    )
    load_w1 = pltpu.make_async_copy(kernel_first, weight_one, local_sem.at[3])
    load_w2 = pltpu.make_async_copy(kernel_second, weight_two, local_sem.at[4])

    def halo_copy(buf, slot, send, recv, d):
        dh, dw = DIRECTIONS[d]
        row_from, row_to, nrow = {-1: (1, rows + 1, 1), 0: (1, 1, rows), 1: (rows, 0, 1)}[dh]
        col_from, col_to, ncol = {
            -1: (PAD, PAD + cols, PAD),
            0: (PAD, PAD, cols),
            1: (cols, 0, PAD),
        }[dw]
        copy = pltpu.make_async_remote_copy(
            src_ref=buf.at[slot, :, pl.ds(row_from, nrow), pl.ds(col_from, ncol), :],
            dst_ref=buf.at[slot, :, pl.ds(row_to, nrow), pl.ds(col_to, ncol), :],
            send_sem=send.at[slot, d],
            recv_sem=recv.at[slot, d],
            device_id={"ha": ha + dh, "wa": wa + dw},
            device_id_type=MESH,
        )
        to_h, to_w = ha + dh, wa + dw
        from_h, from_w = ha - dh, wa - dw
        goes = (to_h >= 0) & (to_h < nha) & (to_w >= 0) & (to_w < nwa)
        comes = (from_h >= 0) & (from_h < nha) & (from_w >= 0) & (from_w < nwa)
        return copy, goes, comes

    def halo(action, buf, slot, send, recv, beside):
        for d in range(len(DIRECTIONS)):
            if (DIRECTIONS[d][0] == 0) not in beside:
                continue
            copy, goes, comes = halo_copy(buf, slot, send, recv, d)
            if action == "start":
                pl.when(goes)(copy.start)
            elif action == "recv":
                pl.when(comes)(copy.wait_recv)
            else:
                pl.when(goes)(copy.wait_send)

    def raw_halo(action, slot, beside=(False, True)):
        halo(action, raw, slot, raw_send, raw_recv, beside)

    def hid_halo(action, slot):
        halo(action, hid_edge, slot, hid_send, hid_recv, (False, True))

    def time_copies(step):
        slot = 2 - step
        parts = ((1, 1), (rows, 1), (2, rows - 2))
        return [
            pltpu.make_async_remote_copy(
                src_ref=raw.at[2, :, pl.ds(first, n), pl.ds(PAD, cols), :],
                dst_ref=raw.at[slot, :, pl.ds(first, n), pl.ds(PAD, cols), :],
                send_sem=time_send.at[step - 1, i],
                recv_sem=time_recv.at[step - 1, i],
                device_id={"ta": ta + step},
                device_id_type=MESH,
            )
            for i, (first, n) in enumerate(parts)
        ]

    steps = [step for step in (1, 2) if step < nta]

    def stat_copy(which, k):
        return pltpu.make_async_remote_copy(
            src_ref=stat_own.at[which],
            dst_ref=stat_in.at[which, k - 1],
            send_sem=stat_send.at[which],
            recv_sem=stat_recv.at[which],
            device_id=place(k),
            device_id_type=MESH,
        )

    def send_stats(which):
        @pl.loop(1, peers)
        def _(k):
            stat_copy(which, k).start()

    def group_total(which):
        pltpu.make_async_copy(stat_in.at[which], stat_in.at[which], stat_recv.at[which]).wait()
        sums = stat_own[which] + jnp.sum(stat_in[which], axis=0)
        lane = lax.broadcasted_iota(jnp.int32, sums.shape, 1)
        for shift in (1, 2):
            low = lax.rem(lane, 2 * shift) < shift
            sums = sums + jnp.where(
                low, pltpu.roll(sums, chans - shift, 1), pltpu.roll(sums, shift, 1)
            )
        return sums

    def scale_of(which, gain):
        sums = group_total(which)
        mean = sums[0:1] / count
        inverse = lax.rsqrt(sums[1:2] / count - mean * mean + EPS)
        return mean, inverse * gain[...]

    def put_stats(which, first, second):
        stat_own[which, 0:1, :] = jnp.sum(first, axis=0, keepdims=True)
        stat_own[which, 1:2, :] = jnp.sum(second, axis=0, keepdims=True)

    def act(value, mean, scale, shift):
        half = (value - mean) * (0.5 * scale) + 0.5 * shift[...]
        return half + half * jnp.tanh(half)

    half_pad = PAD // 2

    def spread(dst, frame, row, left, mid, right):
        left = jnp.where(wa > 0, left, 0.0)
        right = jnp.where(wa < nwa - 1, right, 0.0)
        if row in (0, rows + 1):
            live = (ha > 0) if row == 0 else (ha < nha - 1)
            left, mid, right = (jnp.where(live, value, 0.0) for value in (left, mid, right))
        line[row, 0:half_pad] = left
        line[row, half_pad : half_pad + cols] = mid
        line[row, half_pad + cols : PAD + cols] = right
        before = line[row, half_pad - 1 : half_pad - 1 + cols]
        after = line[row, half_pad + 1 : half_pad + 1 + cols]
        dst[frame, row, :, 0:chans] = before.astype(jnp.bfloat16)
        dst[frame, row, :, chans : 2 * chans] = mid.astype(jnp.bfloat16)
        dst[frame, row, :, 2 * chans :] = after.astype(jnp.bfloat16)

    def edges(buf, slot, f, r):
        left = buf[slot, f, r, 0:PAD].astype(jnp.float32)[half_pad:]
        right = buf[slot, f, r, PAD + cols :].astype(jnp.float32)[:half_pad]
        return left, right

    def middle(buf, slot, f, r):
        return buf[slot, f, r, PAD : PAD + cols].astype(jnp.float32)

    def spread_frames(dst, base, buf, slot, change, own=None):
        @pl.loop(0, nframe)
        def _(f):
            for r in range(rows2):
                left, right = edges(buf, slot, f, r)
                if own is not None and 0 < r < rows + 1:
                    mid = own[slot, f, r - 1]
                else:
                    mid = middle(buf, slot, f, r)
                spread(dst, base + f, r, change(left), change(mid), change(right))

    def spread_plain(dst, base, buf, slot):
        spread_frames(dst, base, buf, slot, lambda value: value)

    def spread_act(dst, base, slot, mean, scale, shift):
        spread_frames(dst, base, raw, slot, lambda value: act(value, mean, scale, shift))

    def spread_hidden(dst, base, slot, mean, scale, shift):
        spread_frames(
            dst, base, hid_edge, slot, lambda value: act(value, mean, scale, shift), hid
        )

    def slab(src, f):
        return jnp.concatenate(
            [src[f, b : b + rows].reshape(rows * cols, 3 * chans) for b in range(3)], axis=1
        )

    def dot(left, right):
        return jnp.dot(left, right, preferred_element_type=jnp.float32)

    def shaped(*pair):
        return [value.reshape(rows, cols, chans) for value in pair]

    def head(src, base, weight):
        both = dot(slab(src, base + 1), jnp.concatenate([weight[1], weight[0]], axis=1))
        one = both[:, :chans] + dot(slab(src, base), weight[0])
        return shaped(one, both[:, chans:])

    def tail(src, base, weight):
        both = dot(slab(src, base + 2), jnp.concatenate([weight[2], weight[1]], axis=1))
        two = both[:, chans:] + dot(slab(src, base + 3), weight[2])
        return shaped(both[:, :chans], two)

    def keep_edges(slot, pair):
        for f, value in enumerate(pair):
            hid_edge[slot, f, 1 : rows + 1, PAD : PAD + cols, :] = value.astype(jnp.bfloat16)

    load_frames.start()

    @pl.when(ta < 2)
    def _():
        load_past.start()

    @pl.when(ta == 0)
    def _():
        load_second.start()

    barrier = pltpu.get_barrier_semaphore()

    @pl.loop(1, peers)
    def _(k):
        pl.semaphore_signal(barrier, inc=1, device_id=place(k), device_id_type=MESH)

    for copy in load_vectors:
        copy.start()
    load_w1.start()
    load_w2.start()
    load_frames.wait()
    first = jnp.zeros((cols, chans), jnp.float32)
    second = jnp.zeros((cols, chans), jnp.float32)
    for f in range(nframe):
        for r in range(rows):
            value = raw[2, f, 1 + r, PAD : PAD + cols, :].astype(jnp.float32)
            first = first + value
            second = second + value * value
    put_stats(0, first, second)
    for copy in load_vectors:
        copy.wait()
    pl.semaphore_wait(barrier, peers - 1)

    for step in steps:

        @pl.when(ta + step < nta)
        def _():
            for copy in time_copies(step):
                copy.start()

    send_stats(0)
    raw_halo("start", 2)

    @pl.when(ta == 0)
    def _():
        load_past.wait()
        raw_halo("start", 1)
        load_second.wait()
        hid_halo("start", 0)

    @pl.when(ta == 1)
    def _():
        load_past.wait()
        raw_halo("start", 0)

    mean_one, scale_one = scale_of(0, gain_first)
    raw_halo("recv", 2)
    spread_act(cols_one, 4, 2, mean_one, scale_one, shift_first)
    load_w1.wait()
    for f, value in enumerate(tail(cols_one, 2, weight_one)):
        hid[1, f] = value + bias_first[...]

    @pl.when(ta == 0)
    def _():
        raw_halo("recv", 1)
        spread_plain(cols_one, 2, raw, 1)

    def past_part():
        for f, value in enumerate(head(cols_one, 0, weight_one)):
            hid[0, f] = value + bias_first[...]

    @pl.when(ta > 0)
    def _():
        def arrive(step):
            for copy in time_copies(step)[:2]:
                copy.wait_recv()
            raw_halo("start", 2 - step, (False,))

        def arrive_all(step):
            time_copies(step)[2].wait_recv()
            raw_halo("start", 2 - step, (True,))

        @pl.when(ta == 1)
        def _():
            raw_halo("recv", 0)
            spread_plain(cols_one, 0, raw, 0)

        arrive(1)

        @pl.when(ta == 1)
        def _():
            past_part()

        arrive_all(1)
        if nta > 2:

            @pl.when(ta > 1)
            def _():
                arrive(2)
                arrive_all(2)
                raw_halo("recv", 0)
                spread_act(cols_one, 0, 0, mean_one, scale_one, shift_first)
                past_part()

        raw_halo("recv", 1)
        spread_act(cols_one, 2, 1, mean_one, scale_one, shift_first)

    pair = head(cols_one, 2, weight_one)
    pair = [value + hid[1, f] for f, value in enumerate(pair)]
    flat = [value.reshape(rows * cols, chans) for value in pair]
    put_stats(1, flat[0] + flat[1], flat[0] * flat[0] + flat[1] * flat[1])
    send_stats(1)
    for f, value in enumerate(pair):
        hid[1, f] = value
    keep_edges(1, pair)
    hid_halo("start", 1)
    load_w2.wait()
    for f in range(nframe):
        total[f] = middle(raw, 2, f, slice(1, rows + 1)) + bias_second[...]

    def carried_part():
        for f, value in enumerate(head(cols_two, 0, weight_two)):
            total[f] += value

    @pl.when(ta > 0)
    def _():
        pair = tail(cols_one, 0, weight_one)
        pair = [value + hid[0, f] for f, value in enumerate(pair)]
        for f, value in enumerate(pair):
            hid[0, f] = value
        keep_edges(0, pair)
        hid_halo("start", 0)

    @pl.when(ta == 0)
    def _():
        hid_halo("recv", 0)
        spread_plain(cols_two, 0, hid_edge, 0)
        carried_part()

    mean_two, scale_two = scale_of(1, gain_second)
    hid_halo("recv", 1)
    spread_hidden(cols_two, 2, 1, mean_two, scale_two, shift_second)
    for f, value in enumerate(tail(cols_two, 0, weight_two)):
        total[f] += value

    @pl.when(ta > 0)
    def _():
        hid_halo("recv", 0)
        spread_hidden(cols_two, 0, 0, mean_two, scale_two, shift_second)
        carried_part()

    for f in range(nframe):
        out[f] = total[f].astype(out.dtype)

    for step in steps:

        @pl.when(ta + step < nta)
        def _():
            for copy in time_copies(step):
                copy.wait_send()

    raw_halo("send", 2)
    raw_halo("send", 1)

    @pl.when(ta > 0)
    def _():
        raw_halo("send", 0)

    hid_halo("send", 1)
    hid_halo("send", 0)
    for which in range(2):
        pltpu.make_async_copy(stat_in.at[which], stat_in.at[which], stat_send.at[which]).wait()


def on_device(
    sizes,
    frames,
    past_first,
    past_second,
    gain_first,
    shift_first,
    kernel_first,
    bias_first,
    gain_second,
    shift_second,
    kernel_second,
    bias_second,
):
    nframe, rows, cols, chans = frames.shape
    nha, nwa, nta = sizes
    peers = nha * nwa * nta
    line = lambda v: v.reshape(1, chans)
    stack = lambda k: k.reshape(3, 9 * chans, chans)
    bf16, f32 = jnp.bfloat16, jnp.float32
    hbm = pl.BlockSpec(memory_space=pltpu.HBM)
    vmem = pl.BlockSpec(memory_space=pltpu.VMEM)
    dma = pltpu.SemaphoreType.DMA
    padded = (rows + 2, cols + 2 * PAD, chans)
    sides = len(DIRECTIONS)
    return pl.pallas_call(
        functools.partial(body, sizes),
        out_shape=jax.ShapeDtypeStruct(frames.shape, bf16),
        in_specs=[hbm] * 11,
        out_specs=vmem,
        scratch_shapes=[
            pltpu.VMEM((6, 1, chans), f32),
            pltpu.VMEM((nframe, rows, cols, chans), f32),
            pltpu.VMEM((3, nframe) + padded, bf16),
            pltpu.VMEM((2, nframe) + padded, bf16),
            pltpu.VMEM((2, nframe, rows, cols, chans), f32),
            pltpu.VMEM((rows + 2, cols + PAD, chans), f32),
            pltpu.VMEM((3 * nframe, rows + 2, cols, 3 * chans), bf16),
            pltpu.VMEM((2 * nframe, rows + 2, cols, 3 * chans), bf16),
            pltpu.VMEM((3, 9 * chans, chans), bf16),
            pltpu.VMEM((3, 9 * chans, chans), bf16),
            pltpu.VMEM((2, 2, chans), f32),
            pltpu.VMEM((2, peers - 1, 2, chans), f32),
            dma((11,)),
            dma((3, sides)),
            dma((3, sides)),
            dma((2, sides)),
            dma((2, sides)),
            dma((2, 3)),
            dma((2, 3)),
            dma((2,)),
            dma((2,)),
        ],
        compiler_params=pltpu.CompilerParams(
            collective_id=0, has_side_effects=True, vmem_limit_bytes=62 * 1024 * 1024
        ),
        cost_estimate=pl.CostEstimate(
            flops=4 * 27 * nframe * rows * cols * chans * chans,
            bytes_accessed=4 * 1024 * 1024,
            transcendentals=4 * nframe * rows * cols * chans,
        ),
    )(
        frames,
        past_first,
        past_second,
        line(gain_first),
        line(shift_first),
        stack(kernel_first),
        line(bias_first),
        line(gain_second),
        line(shift_second),
        stack(kernel_second),
        line(bias_second),
    )


def solution(mesh):
    sizes = tuple(mesh.shape[name] for name in ("ha", "wa", "ta"))
    return jax.shard_map(
        functools.partial(on_device, sizes),
        mesh=mesh,
        in_specs=(
            P(("clips", "ta"), "ha", "wa", None),
            P("clips", "ha", "wa", None),
            P("clips", "ha", "wa", None),
        )
        + (P(),) * 8,
        out_specs=P(("clips", "ta"), "ha", "wa", None),
        check_vma=False,
    )
```

profile of v0, /device:TPU:3, one launch (start us, length us, event | category | flops | bytes accessed | tf_op | source)
XLA Modules:
  0.0 28.8 jit_solution(7531493628792405469)
XLA Ops:
  0.0 27.1 %shard_map.109 = bf16[2,4,128,128]{3,2,1,0:T(8,128)(2,1)} custom-call(bf16[2,4,128,128]{3,2,1,0:T(8,128)(2,1)} %frames.1, bf16[2,4,128,128]{3,2,1,0:T(8,128)(2,1)} %past_first.1, bf16[2,4,128,128]{3,2,1,0:T(8,128)(2,1)} %past_second.1, f32[1,128]{1,0:T(1,128)} %bitcast.10, f32[1,128]{1,0:T(1,128)} %bitcast.11, bf16[3,1152,128]{2,1,0:T(8,128)(2,1)} %bitcast.8, ...), custom_call_target="tpu_custom_call" | custom-call | flops 1811939328 | bytes 4194304 | tf_op jit(solution)/shard_map/pallas_call | solution.py:461
  27.1 1.7 %copy.13 = bf16[2,4,128,128]{3,2,1,0:T(8,128)(2,1)} copy(bf16[2,4,128,128]{3,2,1,0:T(8,128)(2,1)} %shard_map.109) | data formatting | bytes 524288
where the time goes:
time: 28.9 us; the launch traced here: 28.8 us
  Pallas kernels  27.1 us (94%)
  local copies, waits for them, and re-layouts  1.67 us (6%)
    pallas_call x1, Pallas kernels, on_device(): pl.pallas_call(functools.partial(body, sizes), out_shape=jax.ShapeDtypeSt...  27.1 us
    unnamed x1, local copies, waits for them, and re-layouts  1.67 us

commit v1 on v0

--- a/solution.py
+++ b/solution.py
@@ -47,6 +47,8 @@
     hid_recv,
     time_send,
     time_recv,
+    col_send,
+    col_recv,
     stat_send,
     stat_recv,
 ):
@@ -55,16 +57,21 @@
     _, nframe, rows2, width, chans = raw.shape
     rows, cols = rows2 - 2, width - 2 * PAD
     ha, wa, ta = lax.axis_index("ha"), lax.axis_index("wa"), lax.axis_index("ta")
-    me = (ha * nwa + wa) * nta + ta
     count = float(nframe * rows * cols * (chans // G) * peers)
 
+    def ring(at, step, size):
+        return jnp.where(at + step >= size, at + step - size, at + step)
+
     def place(k):
-        other = lax.rem(me + k, peers)
-        return {
-            "ha": other // (nwa * nta),
-            "wa": lax.rem(other // nta, nwa),
-            "ta": lax.rem(other, nta),
-        }
+        dh, dw, dt = k // (nwa * nta), k // nta % nwa, k % nta
+        return {"ha": ring(ha, dh, nha), "wa": ring(wa, dw, nwa), "ta": ring(ta, dt, nta)}
+
+    def each_peer(work):
+        if peers <= 32:
+            for k in range(1, peers):
+                work(k)
+        else:
+            pl.loop(1, peers)(work)
 
     def inner(buf, slot):
         return buf.at[slot, :, pl.ds(1, rows), pl.ds(PAD, cols), :]
@@ -81,7 +88,7 @@
         bias_second_in,
     )
     load_vectors = [
-        pltpu.make_async_copy(ref, vectors.at[i], local_sem.at[5 + i])
+        pltpu.make_async_copy(ref, vectors.at[i, 0], local_sem.at[5 + i])
         for i, ref in enumerate(vector_in)
     ]
     gain_first, shift_first, bias_first, gain_second, shift_second, bias_second = (
@@ -130,9 +137,10 @@
     def hid_halo(action, slot):
         halo(action, hid_edge, slot, hid_send, hid_recv, (False, True))
 
+    row_parts = ((1, 1), (rows, 1), (2, rows - 2))
+
     def time_copies(step):
         slot = 2 - step
-        parts = ((1, 1), (rows, 1), (2, rows - 2))
         return [
             pltpu.make_async_remote_copy(
                 src_ref=raw.at[2, :, pl.ds(first, n), pl.ds(PAD, cols), :],
@@ -142,8 +150,29 @@
                 device_id={"ta": ta + step},
                 device_id_type=MESH,
             )
-            for i, (first, n) in enumerate(parts)
+            for i, (first, n) in enumerate(row_parts)
         ]
+
+    def column_relays(action, part):
+        first, n = row_parts[part]
+        for side, dw in enumerate((-1, 1)):
+            col_from, col_to = (PAD, PAD + cols) if dw < 0 else (cols, 0)
+            copy = pltpu.make_async_remote_copy(
+                src_ref=raw.at[1, :, pl.ds(first, n), pl.ds(col_from, PAD), :],
+                dst_ref=raw.at[1, :, pl.ds(first, n), pl.ds(col_to, PAD), :],
+                send_sem=col_send.at[part, side],
+                recv_sem=col_recv.at[part, side],
+                device_id={"wa": wa + dw},
+                device_id_type=MESH,
+            )
+            goes = (wa + dw >= 0) & (wa + dw < nwa)
+            comes = (wa - dw >= 0) & (wa - dw < nwa)
+            if action == "start":
+                pl.when(goes)(copy.start)
+            elif action == "recv":
+                pl.when(comes)(copy.wait_recv)
+            else:
+                pl.when(goes)(copy.wait_send)
 
     steps = [step for step in (1, 2) if step < nta]
 
@@ -158,9 +187,7 @@
         )
 
     def send_stats(which):
-        @pl.loop(1, peers)
-        def _(k):
-            stat_copy(which, k).start()
+        each_peer(lambda k: stat_copy(which, k).start())
 
     def group_total(which):
         pltpu.make_async_copy(stat_in.at[which], stat_in.at[which], stat_recv.at[which]).wait()
@@ -212,10 +239,10 @@
     def middle(buf, slot, f, r):
         return buf[slot, f, r, PAD : PAD + cols].astype(jnp.float32)
 
-    def spread_frames(dst, base, buf, slot, change, own=None):
+    def spread_frames(dst, base, buf, slot, change, own=None, which=None):
         @pl.loop(0, nframe)
         def _(f):
-            for r in range(rows2):
+            for r in which or range(rows2):
                 left, right = edges(buf, slot, f, r)
                 if own is not None and 0 < r < rows + 1:
                     mid = own[slot, f, r - 1]
@@ -226,8 +253,10 @@
     def spread_plain(dst, base, buf, slot):
         spread_frames(dst, base, buf, slot, lambda value: value)
 
-    def spread_act(dst, base, slot, mean, scale, shift):
-        spread_frames(dst, base, raw, slot, lambda value: act(value, mean, scale, shift))
+    def spread_act(dst, base, slot, mean, scale, shift, which=None):
+        spread_frames(
+            dst, base, raw, slot, lambda value: act(value, mean, scale, shift), None, which
+        )
 
     def spread_hidden(dst, base, slot, mean, scale, shift):
         spread_frames(
@@ -271,9 +300,9 @@
 
     barrier = pltpu.get_barrier_semaphore()
 
-    @pl.loop(1, peers)
-    def _(k):
-        pl.semaphore_signal(barrier, inc=1, device_id=place(k), device_id_type=MESH)
+    each_peer(
+        lambda k: pl.semaphore_signal(barrier, inc=1, device_id=place(k), device_id_type=MESH)
+    )
 
     for copy in load_vectors:
         copy.start()
@@ -306,8 +335,6 @@
     def _():
         load_past.wait()
         raw_halo("start", 1)
-        load_second.wait()
-        hid_halo("start", 0)
 
     @pl.when(ta == 1)
     def _():
@@ -323,6 +350,8 @@
 
     @pl.when(ta == 0)
     def _():
+        load_second.wait()
+        hid_halo("start", 0)
         raw_halo("recv", 1)
         spread_plain(cols_one, 2, raw, 1)
 
@@ -332,39 +361,43 @@
 
     @pl.when(ta > 0)
     def _():
-        def arrive(step):
-            for copy in time_copies(step)[:2]:
-                copy.wait_recv()
-            raw_halo("start", 2 - step, (False,))
-
-        def arrive_all(step):
-            time_copies(step)[2].wait_recv()
-            raw_halo("start", 2 - step, (True,))
-
         @pl.when(ta == 1)
         def _():
             raw_halo("recv", 0)
             spread_plain(cols_one, 0, raw, 0)
 
-        arrive(1)
+        near = time_copies(1)
+        for part in (0, 1):
+            near[part].wait_recv()
+            column_relays("start", part)
+        raw_halo("start", 1, (False,))
 
         @pl.when(ta == 1)
         def _():
             past_part()
 
-        arrive_all(1)
+        def carried(which):
+            spread_act(cols_one, 2, 1, mean_one, scale_one, shift_first, which)
+
+        column_relays("recv", 0)
+        column_relays("recv", 1)
+        carried((1, rows))
+        near[2].wait_recv()
+        column_relays("start", 2)
+        raw_halo("recv", 1, (False,))
+        carried((0, rows + 1))
+        column_relays("recv", 2)
+        carried(tuple(range(2, rows)))
         if nta > 2:
 
             @pl.when(ta > 1)
             def _():
-                arrive(2)
-                arrive_all(2)
+                for copy in time_copies(2):
+                    copy.wait_recv()
+                raw_halo("start", 0)
                 raw_halo("recv", 0)
                 spread_act(cols_one, 0, 0, mean_one, scale_one, shift_first)
                 past_part()
-
-        raw_halo("recv", 1)
-        spread_act(cols_one, 2, 1, mean_one, scale_one, shift_first)
 
     pair = head(cols_one, 2, weight_one)
     pair = [value + hid[1, f] for f, value in enumerate(pair)]
@@ -421,10 +454,16 @@
                 copy.wait_send()
 
     raw_halo("send", 2)
-    raw_halo("send", 1)
+    raw_halo("send", 1, (False,))
+
+    @pl.when(ta == 0)
+    def _():
+        raw_halo("send", 1, (True,))
 
     @pl.when(ta > 0)
     def _():
+        for part in range(3):
+            column_relays("send", part)
         raw_halo("send", 0)
 
     hid_halo("send", 1)
@@ -450,7 +489,7 @@
     nframe, rows, cols, chans = frames.shape
     nha, nwa, nta = sizes
     peers = nha * nwa * nta
-    line = lambda v: v.reshape(1, chans)
+    line = lambda v: v
     stack = lambda k: k.reshape(3, 9 * chans, chans)
     bf16, f32 = jnp.bfloat16, jnp.float32
     hbm = pl.BlockSpec(memory_space=pltpu.HBM)
@@ -483,6 +522,8 @@
             dma((2, sides)),
             dma((2, 3)),
             dma((2, 3)),
+            dma((3, 2)),
+            dma((3, 2)),
             dma((2,)),
             dma((2,)),
         ],

time: 28.9 us -> 28.7 us (level)
  no operation moved by 1% of the time
where the time goes in v1:
time: 28.7 us; the launch traced here: 28.5 us
  Pallas kernels  26.9 us (94%)
  local copies, waits for them, and re-layouts  1.67 us (6%)
    pallas_call x1, Pallas kernels, on_device(): pl.pallas_call(functools.partial(body, sizes), out_shape=jax.ShapeDtypeSt...  26.9 us
    unnamed x1, local copies, waits for them, and re-layouts  1.67 us

profile of v1, /device:TPU:3, one launch (start us, length us, event | category | flops | bytes accessed | tf_op | source)
XLA Modules:
  0.0 28.5 jit_solution(1867097836057041539)
XLA Ops:
  0.0 26.9 %shard_map.109 = bf16[2,4,128,128]{3,2,1,0:T(8,128)(2,1)} custom-call(bf16[2,4,128,128]{3,2,1,0:T(8,128)(2,1)} %frames.1, bf16[2,4,128,128]{3,2,1,0:T(8,128)(2,1)} %past_first.1, bf16[2,4,128,128]{3,2,1,0:T(8,128)(2,1)} %past_second.1, f32[128]{0:T(128)} %gain_first_in.1, f32[128]{0:T(128)} %shift_first_in.1, bf16[3,1152,128]{2,1,0:T(8,128)(2,1)} %bitcast.2, ...), custom_call_target="tpu_custom_call" | custom-call | flops 1811939328 | bytes 4194304 | tf_op jit(solution)/shard_map/pallas_call | solution.py:500
  26.9 1.7 %copy.13 = bf16[2,4,128,128]{3,2,1,0:T(8,128)(2,1)} copy(bf16[2,4,128,128]{3,2,1,0:T(8,128)(2,1)} %shard_map.109) | data formatting | bytes 524288

commit v2 on v1

--- a/solution.py
+++ b/solution.py
@@ -215,6 +215,7 @@
         return half + half * jnp.tanh(half)
 
     half_pad = PAD // 2
+    origin = jnp.minimum(ta, 0)
 
     def spread(dst, frame, row, left, mid, right):
         left = jnp.where(wa > 0, left, 0.0)
@@ -225,8 +226,8 @@
         line[row, 0:half_pad] = left
         line[row, half_pad : half_pad + cols] = mid
         line[row, half_pad + cols : PAD + cols] = right
-        before = line[row, half_pad - 1 : half_pad - 1 + cols]
-        after = line[row, half_pad + 1 : half_pad + 1 + cols]
+        before = line[row, pl.ds(half_pad - 1 + origin, cols)]
+        after = line[row, pl.ds(half_pad + 1 + origin, cols)]
         dst[frame, row, :, 0:chans] = before.astype(jnp.bfloat16)
         dst[frame, row, :, chans : 2 * chans] = mid.astype(jnp.bfloat16)
         dst[frame, row, :, 2 * chans :] = after.astype(jnp.bfloat16)
@@ -341,40 +342,38 @@
         load_past.wait()
         raw_halo("start", 0)
 
+    def past_part():
+        for f, value in enumerate(head(cols_one, 0, weight_one)):
+            hid[0, f] = value + bias_first[...]
+
+    load_w1.wait()
+
+    @pl.when(ta == 0)
+    def _():
+        raw_halo("recv", 1)
+        spread_plain(cols_one, 2, raw, 1)
+        load_second.wait()
+        hid_halo("start", 0)
+
+    @pl.when(ta == 1)
+    def _():
+        raw_halo("recv", 0)
+        spread_plain(cols_one, 0, raw, 0)
+        past_part()
+
     mean_one, scale_one = scale_of(0, gain_first)
     raw_halo("recv", 2)
     spread_act(cols_one, 4, 2, mean_one, scale_one, shift_first)
-    load_w1.wait()
     for f, value in enumerate(tail(cols_one, 2, weight_one)):
         hid[1, f] = value + bias_first[...]
 
-    @pl.when(ta == 0)
-    def _():
-        load_second.wait()
-        hid_halo("start", 0)
-        raw_halo("recv", 1)
-        spread_plain(cols_one, 2, raw, 1)
-
-    def past_part():
-        for f, value in enumerate(head(cols_one, 0, weight_one)):
-            hid[0, f] = value + bias_first[...]
-
     @pl.when(ta > 0)
     def _():
-        @pl.when(ta == 1)
-        def _():
-            raw_halo("recv", 0)
-            spread_plain(cols_one, 0, raw, 0)
-
         near = time_copies(1)
         for part in (0, 1):
             near[part].wait_recv()
             column_relays("start", part)
         raw_halo("start", 1, (False,))
-
-        @pl.when(ta == 1)
-        def _():
-            past_part()
 
         def carried(which):
             spread_act(cols_one, 2, 1, mean_one, scale_one, shift_first, which)

time: 28.7 us -> 28.9 us (level)
  no operation moved by 1% of the time
where the time goes in v2:
time: 28.9 us; the launch traced here: 28.8 us
  Pallas kernels  27.1 us (94%)
  local copies, waits for them, and re-layouts  1.67 us (6%)
    pallas_call x1, Pallas kernels, on_device(): pl.pallas_call(functools.partial(body, sizes), out_shape=jax.ShapeDtypeSt...  27.1 us
    unnamed x1, local copies, waits for them, and re-layouts  1.67 us

profile of v2, /device:TPU:3, one launch (start us, length us, event | category | flops | bytes accessed | tf_op | source)
XLA Modules:
  0.0 28.8 jit_solution(6788236267370369509)
XLA Ops:
  0.0 27.1 %shard_map.109 = bf16[2,4,128,128]{3,2,1,0:T(8,128)(2,1)} custom-call(bf16[2,4,128,128]{3,2,1,0:T(8,128)(2,1)} %frames.1, bf16[2,4,128,128]{3,2,1,0:T(8,128)(2,1)} %past_first.1, bf16[2,4,128,128]{3,2,1,0:T(8,128)(2,1)} %past_second.1, f32[128]{0:T(128)} %gain_first_in.1, f32[128]{0:T(128)} %shift_first_in.1, bf16[3,1152,128]{2,1,0:T(8,128)(2,1)} %bitcast.2, ...), custom_call_target="tpu_custom_call" | custom-call | flops 1811939328 | bytes 4194304 | tf_op jit(solution)/shard_map/pallas_call | solution.py:499
  27.1 1.7 %copy.13 = bf16[2,4,128,128]{3,2,1,0:T(8,128)(2,1)} copy(bf16[2,4,128,128]{3,2,1,0:T(8,128)(2,1)} %shard_map.109) | data formatting | bytes 524288

commit v3 on v1

--- a/solution.py
+++ b/solution.py
@@ -320,6 +320,7 @@
     for copy in load_vectors:
         copy.wait()
     pl.semaphore_wait(barrier, peers - 1)
+    send_stats(0)
 
     for step in steps:
 
@@ -328,7 +329,6 @@
             for copy in time_copies(step):
                 copy.start()
 
-    send_stats(0)
     raw_halo("start", 2)
 
     @pl.when(ta == 0)

time: 28.7 us -> 24.9 us (0.87)
  the two profiles are of different devices: /device:TPU:3 before, /device:TPU:0 now
where the time goes in v3:
time: 24.9 us; the launch traced here: 24.8 us
  Pallas kernels  23.1 us (93%)
  local copies, waits for them, and re-layouts  1.67 us (7%)
    pallas_call x1, Pallas kernels, on_device(): pl.pallas_call(functools.partial(body, sizes), out_shape=jax.ShapeDtypeSt...  23.1 us
    unnamed x1, local copies, waits for them, and re-layouts  1.67 us

profile of v3, /device:TPU:0, one launch (start us, length us, event | category | flops | bytes accessed | tf_op | source)
XLA Modules:
  0.0 24.8 jit_solution(3813639792923125346)
XLA Ops:
  0.0 23.1 %shard_map.109 = bf16[2,4,128,128]{3,2,1,0:T(8,128)(2,1)} custom-call(bf16[2,4,128,128]{3,2,1,0:T(8,128)(2,1)} %frames.1, bf16[2,4,128,128]{3,2,1,0:T(8,128)(2,1)} %past_first.1, bf16[2,4,128,128]{3,2,1,0:T(8,128)(2,1)} %past_second.1, f32[128]{0:T(128)} %gain_first_in.1, f32[128]{0:T(128)} %shift_first_in.1, bf16[3,1152,128]{2,1,0:T(8,128)(2,1)} %bitcast.2, ...), custom_call_target="tpu_custom_call" | custom-call | flops 1811939328 | bytes 4194304 | tf_op jit(solution)/shard_map/pallas_call | solution.py:500
  23.1 1.7 %copy.13 = bf16[2,4,128,128]{3,2,1,0:T(8,128)(2,1)} copy(bf16[2,4,128,128]{3,2,1,0:T(8,128)(2,1)} %shard_map.109) | data formatting | bytes 524288
